TPU v7x, 32 devices: a whole 2x2x4 slice. The times are simulated.
32 devices in a mesh: tunnel: 8 (over y, x, core), width: 4 (over z).
Axes of the slice: x: 2, y: 2, z: 4, core: 2. Of those that a mesh axis runs over, the one named last changes fastest.
Arguments:
- source: float32 [512, 128, 512], P('tunnel', 'width'), may hold values from -6 to 6
- initial: float32 [512, 128, 512], P('tunnel', 'width'), may hold values from -6 to 6
- diffusivity: float32 [512, 128, 512], P('tunnel', 'width'), may hold values from 0.5 to 2
- reaction: float32 [512, 128, 512], P('tunnel', 'width'), may hold values from 0.05 to 0.5
Outputs:
- smoothed: float32 [512, 128, 512], P('tunnel', 'width')
- coarse_residual: float32 [256, 64, 256], P('tunnel')
All inputs are finite; a program needn't handle non-finite values.
Results may differ from a plain program's by a relative error of at most 0.00013.
Values sent between devices are 32-bit elements; how exact they have to be, the bound alone decides.
A program may use at most 192 MiB of HBM per device.

v0:
```python
import functools

import jax
import jax.numpy as jnp
from jax import lax
from jax.experimental import pallas as pl
from jax.experimental.pallas import tpu as pltpu
from jax.sharding import PartitionSpec as P

PASSES = 4
CHUNKS = 4
EDGE = CHUNKS
TOP = 8

relax_weight = 0.8
settle_rate = 0.5
MESH = pl.DeviceIdType.MESH


def kernel(
    n_tunnel,
    n_width,
    source,
    initial,
    diffusivity,
    reaction,
    smoothed,
    coarse,
    va,
    vb,
    src,
    dif,
    rea,
    rec,
    ys,
    yr,
    resid,
    table,
    q,
    yb,
    ycs,
    ycr,
    cz,
    x_send,
    x_recv,
    y_send,
    y_recv,
    q_sem,
    c_send,
    c_recv,
    g_send,
    g_recv,
    in_sem,
    v_sem,
    out_sem,
    own_sem,
):
    planes, rows, height = source.shape
    span = planes // CHUNKS
    tiles = rows // 8
    half = rows // 2
    low = height // 2
    per = span // 2
    t_me = lax.axis_index("tunnel")
    w_me = lax.axis_index("width")
    t_has = (t_me > 0, t_me < n_tunnel - 1)
    w_has = (w_me > 0, w_me < n_width - 1)
    t_to = (
        (jnp.maximum(t_me - 1, 0), w_me),
        (jnp.minimum(t_me + 1, n_tunnel - 1), w_me),
    )
    w_to = (
        (t_me, jnp.maximum(w_me - 1, 0)),
        (t_me, jnp.minimum(w_me + 1, n_width - 1)),
    )
    bufs = (va, vb)
    cells = pl.ds(TOP, rows)

    def bounds(c):
        first = max(span * c - 1, 0)
        last = planes if c == CHUNKS - 1 else span * c + span - 1
        return first, last - first

    load_v = pltpu.make_async_copy(initial, va.at[pl.ds(1, planes), cells, :], v_sem)
    load_v.start()
    loads = {}
    for c in (CHUNKS - 1, 0) + tuple(range(CHUNKS - 2, 0, -1)):
        first, count = bounds(c)
        for a, (hbm, mem) in enumerate(((source, src), (diffusivity, dif), (reaction, rea))):
            loads[a, c] = pltpu.make_async_copy(
                hbm.at[pl.ds(first, count)], mem.at[pl.ds(first, count)], in_sem.at[a, c]
            )
            loads[a, c].start()

    barrier = pltpu.get_barrier_semaphore()
    for d in range(2):

        @pl.when(t_has[d])
        def _():
            pl.semaphore_signal(barrier, inc=1, device_id=t_to[d], device_id_type=MESH)

    for d in range(1, n_width):
        peer = lax.rem(w_me + d, n_width)
        pl.semaphore_signal(barrier, inc=1, device_id=(t_me, peer), device_id_type=MESH)

    for d in range(2):

        @pl.when(jnp.logical_not(t_has[d]))
        def _():
            side = 0 if d == 0 else planes + 1
            for buf in bufs:
                buf[side, cells, :] = jnp.zeros((rows, height), jnp.float32)
            if d == 0:
                q[0] = jnp.zeros((rows, low), jnp.float32)

        @pl.when(jnp.logical_not(w_has[d]))
        def _():
            for k in range(PASSES + 1):
                yr[k, d] = jnp.zeros(yr.shape[2:], jnp.float32)
            if d == 0:
                ycr[...] = jnp.zeros(ycr.shape, jnp.float32)

    fine = lax.broadcasted_iota(jnp.int32, (height, low), 0)
    gap = fine - 2 * lax.broadcasted_iota(jnp.int32, (height, low), 1)
    weight = jnp.where(gap == 0, 0.5, jnp.where((gap == 1) | (gap == -1), 0.25, 0.0))
    table[...] = weight.astype(jnp.float32).astype(jnp.bfloat16)

    beside = jnp.where(t_has[0], 1, 0) + jnp.where(t_has[1], 1, 0)
    pl.semaphore_wait(barrier, n_width - 1 + beside)

    def x_copy(k, d):
        buf = bufs[k % 2]
        mine, theirs = (1, planes + 1) if d == 0 else (planes, 0)
        return pltpu.make_async_remote_copy(
            src_ref=buf.at[mine, cells, :],
            dst_ref=buf.at[theirs, cells, :],
            send_sem=x_send.at[k, d],
            recv_sem=x_recv.at[k, 1 - d],
            device_id=t_to[d],
            device_id_type=MESH,
        )

    def y_copy(k, d, c):
        if k == 0:
            part = pl.ds(0, ys.shape[2])
        elif c == EDGE:
            part = pl.ds(planes, 8)
        else:
            part = pl.ds(span * c, span)
        return pltpu.make_async_remote_copy(
            src_ref=ys.at[k, d, part, :],
            dst_ref=yr.at[k, 1 - d, part, :],
            send_sem=y_send.at[k, d, c],
            recv_sem=y_recv.at[k, 1 - d, c],
            device_id=w_to[d],
            device_id_type=MESH,
        )

    def start_x(k):
        for d in range(2):

            @pl.when(t_has[d])
            def _():
                x_copy(k, d).start()

    def sent_x(k):
        for d in range(2):

            @pl.when(t_has[d])
            def _():
                x_copy(k, d).wait_send()

    def got_x(k):
        for d in range(2):

            @pl.when(t_has[d])
            def _():
                x_copy(k, 1 - d).wait_recv()

    def start_y(k, c):
        for d in range(2):

            @pl.when(w_has[d])
            def _():
                y_copy(k, d, c).start()

    def sent_y(k, c):
        for d in range(2):

            @pl.when(w_has[d])
            def _():
                y_copy(k, d, c).wait_send()

    def got_y(k, c):
        for d in range(2):

            @pl.when(w_has[d])
            def _():
                y_copy(k, 1 - d, c).wait_recv()

    lane = lax.broadcasted_iota(jnp.int32, (8, 128), 1)

    def neighbours(v, p, t):
        here = pl.ds(TOP + 8 * t, 8)
        centre = v[p, here, :]
        beside = (
            v[p - 1, here, :]
            + v[p + 1, here, :]
            + (v[p, pl.ds(TOP + 8 * t - 1, 8), :] + v[p, pl.ds(TOP + 8 * t + 1, 8), :])
        )
        upper = pltpu.roll(centre, height - 1, 1)
        lower = pltpu.roll(centre, 1, 1)
        cut = height - 128
        upper = jnp.concatenate(
            [upper[:, :cut], jnp.where(lane == 127, 0.0, upper[:, cut:])], axis=1
        )
        lower = jnp.concatenate(
            [jnp.where(lane == 0, 0.0, lower[:, :128]), lower[:, 128:]], axis=1
        )
        return centre, 2.5 * beside + 0.5 * (upper + lower), upper

    def put_halo(k, p, row):
        v = bufs[k % 2]
        v[p, TOP - 1 : TOP, :] = yr[k, 0, pl.ds(row, 1), :]
        v[p, TOP + rows : TOP + rows + 1, :] = yr[k, 1, pl.ds(row, 1), :]

    def smooth_plane(k, p, row):
        v, new = bufs[(k - 1) % 2], bufs[k % 2]
        put_halo(k - 1, p, row)
        for t in range(tiles):
            at = pl.ds(8 * t, 8)
            centre, beside, upper = neighbours(v, p, t)
            spread = dif[p - 1, at, :]
            if k == 1:
                factor = relax_weight / (rea[p - 1, at, :] + 11.0 * spread + settle_rate)
                rec[p - 1, at, :] = factor
            else:
                factor = rec[p - 1, at, :]
            off = src[p - 1, at, :] + spread * beside + settle_rate * upper
            out = (1.0 - relax_weight) * centre + factor * off
            new[p, pl.ds(TOP + 8 * t, 8), :] = out
            if t == 0:
                ys[k, 0, pl.ds(row, 1), :] = out[0:1, :]
            if t == tiles - 1:
                ys[k, 1, pl.ds(row, 1), :] = out[7:8, :]

    def residual_plane(p, row, slot):
        v = bufs[PASSES % 2]
        put_halo(PASSES, p, row)
        for t in range(tiles):
            at = pl.ds(8 * t, 8)
            centre, beside, upper = neighbours(v, p, t)
            spread = dif[p - 1, at, :]
            diagonal = rea[p - 1, at, :] + 11.0 * spread + settle_rate
            resid[slot, at, :] = (
                src[p - 1, at, :]
                - diagonal * centre
                + spread * beside
                + settle_rate * upper
            )

    def restrict_height(count):
        r = resid[0:count].reshape(count * rows, height)
        hi = r.astype(jnp.bfloat16)
        lo = (r - hi.astype(jnp.float32)).astype(jnp.bfloat16)
        t = table[...]
        out = jnp.dot(hi, t, preferred_element_type=jnp.float32) + jnp.dot(
            lo, t, preferred_element_type=jnp.float32
        )
        return out.reshape(count, rows, low)

    load_v.wait()
    start_x(0)

    @pl.loop(1, planes + 1)
    def _(p):
        ys[0, 0, pl.ds(p, 1), :] = va[p, TOP : TOP + 1, :]
        ys[0, 1, pl.ds(p, 1), :] = va[p, TOP + rows - 1 : TOP + rows, :]

    ys[0, 0, planes + 1 : planes + 2, :] = va[1, TOP : TOP + 1, :]
    ys[0, 1, planes + 1 : planes + 2, :] = va[1, TOP + rows - 1 : TOP + rows, :]
    start_y(0, EDGE)

    order = tuple(range(CHUNKS - 1, -1, -1))
    stores = {}
    for k in range(1, PASSES + 1):
        if k >= 2:
            sent_x(k - 2)
        if k == 1:
            for c in (CHUNKS - 1, 0):
                for a in range(3):
                    loads[a, c].wait()
        got_x(k - 1)
        got_y(k - 1, EDGE)
        smooth_plane(k, planes, planes)
        smooth_plane(k, 1, planes + 1)
        start_x(k)
        start_y(k, EDGE)
        for c in order:
            if k == 1:
                if 0 < c < CHUNKS - 1:
                    for a in range(3):
                        loads[a, c].wait()
            else:
                got_y(k - 1, c)

            @pl.loop(max(span * c, 2), span * c + span)
            def _(p):
                smooth_plane(k, p, p)

            start_y(k, c)
            if k == PASSES:
                first, count = bounds(c)
                stores[c] = pltpu.make_async_copy(
                    bufs[k % 2].at[pl.ds(first + 1, count), cells, :],
                    smoothed.at[pl.ds(first, count)],
                    out_sem.at[c],
                )
                stores[c].start()

    def q_copy():
        return pltpu.make_async_remote_copy(
            src_ref=q.at[planes],
            dst_ref=q.at[0],
            send_sem=q_sem.at[0],
            recv_sem=q_sem.at[1],
            device_id=t_to[1],
            device_id_type=MESH,
        )

    def c_copy(c):
        part = pl.ds(per * c, per)
        return pltpu.make_async_remote_copy(
            src_ref=ycs.at[part, :],
            dst_ref=ycr.at[part, :],
            send_sem=c_send.at[c],
            recv_sem=c_recv.at[c],
            device_id=w_to[1],
            device_id_type=MESH,
        )

    def g_copy(c, owner, peer, d):
        part = pl.ds(per * c, per)
        return pltpu.make_async_remote_copy(
            src_ref=cz.at[part],
            dst_ref=coarse.at[part, pl.ds(pl.multiple_of(owner * half, 8), half), :],
            send_sem=g_send.at[d, c],
            recv_sem=g_recv.at[owner, c],
            device_id=(t_me, peer),
            device_id_type=MESH,
        )

    def own_copy(c):
        part = pl.ds(per * c, per)
        return pltpu.make_async_copy(
            cz.at[part],
            coarse.at[part, pl.ds(pl.multiple_of(w_me * half, 8), half), :],
            own_sem.at[c],
        )

    def finish(c):
        @pl.when(w_has[0])
        def _():
            c_copy(c).wait_recv()

        @pl.loop(per * c, per * c + per)
        def _(i):
            rim = ycr[pl.ds(i, 1), :]
            for h in range(low // 128):
                yb[i, h, TOP - 1 : TOP, :] = rim[:, 128 * h : 128 * h + 128]
                before = yb[i, h, pl.ds(TOP - 1, half, 2), :]
                middle = yb[i, h, pl.ds(TOP, half, 2), :]
                after = yb[i, h, pl.ds(TOP + 1, half, 2), :]
                cz[i, :, 128 * h : 128 * h + 128] = 0.25 * (before + after) + 0.5 * middle

        own_copy(c).start()
        for d in range(1, n_width):
            g_copy(c, w_me, lax.rem(w_me + d, n_width), d).start()

    got_x(PASSES)
    got_y(PASSES, EDGE)
    residual_plane(planes, planes, 0)
    q[planes] = restrict_height(1)[0]

    @pl.when(t_has[1])
    def _():
        q_copy().start()

    for c in order:
        got_y(PASSES, c)
        if c == 0:
            residual_plane(1, planes + 1, 1)

        @pl.loop(max(span * c, 2), span * c + span)
        def _(p):
            residual_plane(p, p, p - span * c)

        skip = 1 if c == 0 else 0
        q[span * c + skip : span * c + span] = restrict_height(span)[skip:]
        if c == 0:

            @pl.when(t_has[0])
            def _():
                q_copy().wait_recv()

        @pl.loop(per * c, per * c + per)
        def _(i):
            y = 0.25 * (q[2 * i] + q[2 * i + 2]) + 0.5 * q[2 * i + 1]
            for h in range(low // 128):
                yb[i, h, pl.ds(TOP, rows), :] = y[:, 128 * h : 128 * h + 128]
            ycs[pl.ds(i, 1), :] = y[rows - 1 : rows, :]

        @pl.when(w_has[1])
        def _():
            c_copy(c).start()

        if c < CHUNKS - 1:
            finish(c + 1)
    finish(0)

    for k in (PASSES - 1, PASSES):
        sent_x(k)
    for k in range(PASSES + 1):
        for c in (EDGE,) if k == 0 else range(CHUNKS + 1):
            sent_y(k, c)

    @pl.when(t_has[1])
    def _():
        q_copy().wait_send()

    for c in range(CHUNKS):
        stores[c].wait()
        own_copy(c).wait()

        @pl.when(w_has[1])
        def _():
            c_copy(c).wait_send()

        for d in range(1, n_width):
            peer = lax.rem(w_me + d, n_width)
            g_copy(c, w_me, peer, d).wait_send()
            g_copy(c, peer, peer, d).wait_recv()


def solution(mesh):
    n_tunnel, n_width = mesh.shape["tunnel"], mesh.shape["width"]

    def per_device(source, initial, diffusivity, reaction):
        planes, rows, height = source.shape
        low, half = height // 2, rows // 2
        f32 = jnp.float32
        field = (planes, rows, height)
        padded = (planes + 2, rows + 2 * TOP, height)
        columns = (PASSES + 1, 2, planes + 8, height)
        dma = pltpu.SemaphoreType.DMA
        return pl.pallas_call(
            functools.partial(kernel, n_tunnel, n_width),
            out_shape=(
                jax.ShapeDtypeStruct(field, f32),
                jax.ShapeDtypeStruct((planes // 2, half * n_width, low), f32),
            ),
            in_specs=[pl.BlockSpec(memory_space=pl.ANY)] * 4,
            out_specs=(pl.BlockSpec(memory_space=pl.ANY),) * 2,
            scratch_shapes=[
                pltpu.VMEM(padded, f32),
                pltpu.VMEM(padded, f32),
                pltpu.VMEM(field, f32),
                pltpu.VMEM(field, f32),
                pltpu.VMEM(field, f32),
                pltpu.VMEM(field, f32),
                pltpu.VMEM(columns, f32),
                pltpu.VMEM(columns, f32),
                pltpu.VMEM((planes // CHUNKS, rows, height), f32),
                pltpu.VMEM((height, low), jnp.bfloat16),
                pltpu.VMEM((planes + 1, rows, low), f32),
                pltpu.VMEM((planes // 2, low // 128, rows + TOP, 128), f32),
                pltpu.VMEM((planes // 2, low), f32),
                pltpu.VMEM((planes // 2, low), f32),
                pltpu.VMEM((planes // 2, half, low), f32),
                dma((PASSES + 1, 2)),
                dma((PASSES + 1, 2)),
                dma((PASSES + 1, 2, CHUNKS + 1)),
                dma((PASSES + 1, 2, CHUNKS + 1)),
                dma((2,)),
                dma((CHUNKS,)),
                dma((CHUNKS,)),
                dma((n_width, CHUNKS)),
                dma((n_width, CHUNKS)),
                dma((3, CHUNKS)),
                dma(()),
                dma((CHUNKS,)),
                dma((CHUNKS,)),
            ],
            compiler_params=pltpu.CompilerParams(
                collective_id=0, has_side_effects=True, vmem_limit_bytes=58 * 2**20
            ),
        )(source, initial, diffusivity, reaction)

    return jax.shard_map(
        per_device,
        mesh=mesh,
        in_specs=(P("tunnel", "width", None),) * 4,
        out_specs=(P("tunnel", "width", None), P("tunnel", None, None)),
        check_vma=False,
    )
```

profile of v0, /device:TPU:0, one launch (start us, length us, event | category | flops | bytes accessed | tf_op | source)
XLA Modules:
  0.0 101.5 jit_solution(5187235322140078773)
XLA Ops:
  0.6 94.4 %shard_map.59 = (f32[64,32,512]{2,1,0:T(8,128)}, f32[32,64,256]{2,1,0:T(8,128)}) custom-call(f32[64,32,512]{2,1,0:T(8,128)} %source.1, f32[64,32,512]{2,1,0:T(8,128)} %initial.1, f32[64,32,512]{2,1,0:T(8,128)} %diffusivity.1, f32[64,32,512]{2,1,0:T(8,128)} %reaction.1), custom_call_target="tpu_custom_call" | custom-call | tf_op jit(solution)/shard_map/pallas_call | solution.py:456
  95.0 0.0 copy-start
  95.0 5.2 %copy.8 = f32[64,32,512]{2,1,0:T(8,128)} copy(f32[64,32,512]{2,1,0:T(8,128)} %get-tuple-element.4) | data formatting | bytes 8388608
  100.2 0.0 copy-done
  100.2 1.3 %copy.9 = f32[32,64,256]{2,1,0:T(8,128)} copy(f32[32,64,256]{2,1,0:T(8,128)S(1)} %copy-done) | data formatting | bytes 4194304
Async XLA Ops:
  95.0 5.2 %copy-start = (f32[32,64,256]{2,1,0:T(8,128)S(1)}, f32[32,64,256]{2,1,0:T(8,128)}, u32[]{:S(2)}) copy-start(f32[32,64,256]{2,1,0:T(8,128)} %get-tuple-element.5) | copy-start | bytes 6291460
where the time goes:
time: 102 us
  Pallas kernels  94.4 us (93%)
  local copies, waits for them, and re-layouts  6.48 us (6%)
    pallas_call x1, Pallas kernels, per_device(): pl.pallas_call(functools.partial(kernel, n_tunnel, n_width), out_shape=(j...  94.4 us
    unnamed x4, local copies, waits for them, and re-layouts  6.48 us

commit v1 on v0

--- a/solution.py
+++ b/solution.py
@@ -99,9 +99,9 @@
         def _():
             pl.semaphore_signal(barrier, inc=1, device_id=t_to[d], device_id_type=MESH)
 
-    for d in range(1, n_width):
-        peer = lax.rem(w_me + d, n_width)
-        pl.semaphore_signal(barrier, inc=1, device_id=(t_me, peer), device_id_type=MESH)
+        @pl.when(w_has[d])
+        def _():
+            pl.semaphore_signal(barrier, inc=1, device_id=w_to[d], device_id_type=MESH)
 
     for d in range(2):
 
@@ -125,8 +125,8 @@
     weight = jnp.where(gap == 0, 0.5, jnp.where((gap == 1) | (gap == -1), 0.25, 0.0))
     table[...] = weight.astype(jnp.float32).astype(jnp.bfloat16)
 
-    beside = jnp.where(t_has[0], 1, 0) + jnp.where(t_has[1], 1, 0)
-    pl.semaphore_wait(barrier, n_width - 1 + beside)
+    beside = sum(jnp.where(has, 1, 0) for has in t_has + w_has)
+    pl.semaphore_wait(barrier, beside)
 
     def x_copy(k, d):
         buf = bufs[k % 2]
@@ -208,14 +208,15 @@
             + v[p + 1, here, :]
             + (v[p, pl.ds(TOP + 8 * t - 1, 8), :] + v[p, pl.ds(TOP + 8 * t + 1, 8), :])
         )
-        upper = pltpu.roll(centre, height - 1, 1)
-        lower = pltpu.roll(centre, 1, 1)
-        cut = height - 128
+        parts = [centre[:, z : z + 128] for z in range(0, height, 128)]
+        down = [pltpu.roll(part, 127, 1) for part in parts] + [0.0]
+        up = [0.0] + [pltpu.roll(part, 1, 1) for part in parts]
+        count = len(parts)
         upper = jnp.concatenate(
-            [upper[:, :cut], jnp.where(lane == 127, 0.0, upper[:, cut:])], axis=1
+            [jnp.where(lane == 127, down[j + 1], down[j]) for j in range(count)], axis=1
         )
         lower = jnp.concatenate(
-            [jnp.where(lane == 0, 0.0, lower[:, :128]), lower[:, 128:]], axis=1
+            [jnp.where(lane == 0, up[j], up[j + 1]) for j in range(count)], axis=1
         )
         return centre, 2.5 * beside + 0.5 * (upper + lower), upper
 
@@ -339,14 +340,15 @@
             device_id_type=MESH,
         )
 
-    def g_copy(c, owner, peer, d):
+    def g_copy(c, owner, d, mine):
         part = pl.ds(per * c, per)
+        place = coarse.at[part, pl.ds(pl.multiple_of(owner * half, 8), half), :]
         return pltpu.make_async_remote_copy(
-            src_ref=cz.at[part],
-            dst_ref=coarse.at[part, pl.ds(pl.multiple_of(owner * half, 8), half), :],
-            send_sem=g_send.at[d, c],
+            src_ref=cz.at[part] if mine else place,
+            dst_ref=place,
+            send_sem=g_send.at[d, owner, c],
             recv_sem=g_recv.at[owner, c],
-            device_id=(t_me, peer),
+            device_id=w_to[d],
             device_id_type=MESH,
         )
 
@@ -374,8 +376,11 @@
                 cz[i, :, 128 * h : 128 * h + 128] = 0.25 * (before + after) + 0.5 * middle
 
         own_copy(c).start()
-        for d in range(1, n_width):
-            g_copy(c, w_me, lax.rem(w_me + d, n_width), d).start()
+        for d in range(2):
+
+            @pl.when(w_has[d])
+            def _():
+                g_copy(c, w_me, d, True).start()
 
     got_x(PASSES)
     got_y(PASSES, EDGE)
@@ -418,6 +423,19 @@
             finish(c + 1)
     finish(0)
 
+    for step in range(1, n_width):
+        for c in order:
+            for d in range(2):
+                owner = w_me - step if d == 1 else w_me + step
+
+                @pl.when(owner >= 0 if d == 1 else owner < n_width)
+                def _():
+                    g_copy(c, owner, d, False).wait_recv()
+
+                    @pl.when(w_has[d])
+                    def _():
+                        g_copy(c, owner, d, False).start()
+
     for k in (PASSES - 1, PASSES):
         sent_x(k)
     for k in range(PASSES + 1):
@@ -436,10 +454,13 @@
         def _():
             c_copy(c).wait_send()
 
-        for d in range(1, n_width):
-            peer = lax.rem(w_me + d, n_width)
-            g_copy(c, w_me, peer, d).wait_send()
-            g_copy(c, peer, peer, d).wait_recv()
+        for owner in range(n_width):
+            for d in range(2):
+                goes = owner <= w_me if d == 1 else owner >= w_me
+
+                @pl.when(jnp.logical_and(w_has[d], goes))
+                def _():
+                    g_copy(c, owner, d, False).wait_send()
 
 
 def solution(mesh):
@@ -484,7 +505,7 @@
                 dma((2,)),
                 dma((CHUNKS,)),
                 dma((CHUNKS,)),
-                dma((n_width, CHUNKS)),
+                dma((2, n_width, CHUNKS)),
                 dma((n_width, CHUNKS)),
                 dma((3, CHUNKS)),
                 dma(()),

time: 102 us -> 91.8 us (0.900)
  Pallas kernels: 94.4 us -> 84.5 us
    pallas_call x1, Pallas kernels: 94.4 us -> 84.5 us  [per_device(): pl.pallas_call(functools.partial(kernel, n_tunnel, n_width), out_shape=(j...]
where the time goes in v1:
time: 91.8 us; the launch traced here: 91.6 us
  Pallas kernels  84.5 us (92%)
  local copies, waits for them, and re-layouts  6.48 us (7%)
    pallas_call x1, Pallas kernels, per_device(): pl.pallas_call(functools.partial(kernel, n_tunnel, n_width), out_shape=(j...  84.5 us
    unnamed x4, local copies, waits for them, and re-layouts  6.48 us

profile of v1, /device:TPU:0, one launch (start us, length us, event | category | flops | bytes accessed | tf_op | source)
XLA Modules:
  0.0 91.6 jit_solution(6912847730683982640)
XLA Ops:
  0.6 84.5 %shard_map.59 = (f32[64,32,512]{2,1,0:T(8,128)}, f32[32,64,256]{2,1,0:T(8,128)}) custom-call(f32[64,32,512]{2,1,0:T(8,128)} %source.1, f32[64,32,512]{2,1,0:T(8,128)} %initial.1, f32[64,32,512]{2,1,0:T(8,128)} %diffusivity.1, f32[64,32,512]{2,1,0:T(8,128)} %reaction.1), custom_call_target="tpu_custom_call" | custom-call | tf_op jit(solution)/shard_map/pallas_call | solution.py:477
  85.2 0.0 copy-start
  85.2 5.2 %copy.8 = f32[64,32,512]{2,1,0:T(8,128)} copy(f32[64,32,512]{2,1,0:T(8,128)} %get-tuple-element.4) | data formatting | bytes 8388608
  90.3 0.0 copy-done
  90.3 1.3 %copy.9 = f32[32,64,256]{2,1,0:T(8,128)} copy(f32[32,64,256]{2,1,0:T(8,128)S(1)} %copy-done) | data formatting | bytes 4194304
Async XLA Ops:
  85.2 5.2 %copy-start = (f32[32,64,256]{2,1,0:T(8,128)S(1)}, f32[32,64,256]{2,1,0:T(8,128)}, u32[]{:S(2)}) copy-start(f32[32,64,256]{2,1,0:T(8,128)} %get-tuple-element.5) | copy-start | bytes 6291460

commit v2 on v1

--- a/solution.py
+++ b/solution.py
@@ -225,9 +225,13 @@
         v[p, TOP - 1 : TOP, :] = yr[k, 0, pl.ds(row, 1), :]
         v[p, TOP + rows : TOP + rows + 1, :] = yr[k, 1, pl.ds(row, 1), :]
 
+    def put_halos(k, c):
+        @pl.loop(max(span * c, 2), span * c + span, unroll=2)
+        def _(p):
+            put_halo(k, p, p)
+
     def smooth_plane(k, p, row):
         v, new = bufs[(k - 1) % 2], bufs[k % 2]
-        put_halo(k - 1, p, row)
         for t in range(tiles):
             at = pl.ds(8 * t, 8)
             centre, beside, upper = neighbours(v, p, t)
@@ -247,7 +251,6 @@
 
     def residual_plane(p, row, slot):
         v = bufs[PASSES % 2]
-        put_halo(PASSES, p, row)
         for t in range(tiles):
             at = pl.ds(8 * t, 8)
             centre, beside, upper = neighbours(v, p, t)
@@ -270,6 +273,132 @@
         )
         return out.reshape(count, rows, low)
 
+    order = tuple(range(CHUNKS - 1, -1, -1))
+
+    def q_copy():
+        return pltpu.make_async_remote_copy(
+            src_ref=q.at[planes],
+            dst_ref=q.at[0],
+            send_sem=q_sem.at[0],
+            recv_sem=q_sem.at[1],
+            device_id=t_to[1],
+            device_id_type=MESH,
+        )
+
+    def c_copy(c):
+        return pltpu.make_async_remote_copy(
+            src_ref=ycs.at[c],
+            dst_ref=ycr.at[c],
+            send_sem=c_send.at[c],
+            recv_sem=c_recv.at[c],
+            device_id=w_to[1],
+            device_id_type=MESH,
+        )
+
+    def g_copy(c, owner, d, mine):
+        part = pl.ds(per * c, per)
+        place = coarse.at[part, pl.ds(pl.multiple_of(owner * half, 8), half), :]
+        return pltpu.make_async_remote_copy(
+            src_ref=cz.at[part] if mine else place,
+            dst_ref=place,
+            send_sem=g_send.at[d, owner, c],
+            recv_sem=g_recv.at[owner, c],
+            device_id=w_to[d],
+            device_id_type=MESH,
+        )
+
+    def own_copy(c):
+        part = pl.ds(per * c, per)
+        return pltpu.make_async_copy(
+            cz.at[part],
+            coarse.at[part, pl.ds(pl.multiple_of(w_me * half, 8), half), :],
+            own_sem.at[c],
+        )
+
+    def finish(c):
+        @pl.when(w_has[0])
+        def _():
+            c_copy(c).wait_recv()
+
+        @pl.loop(per * c, per * c + per)
+        def _(i):
+            rim = ycr[c, pl.ds(i - per * c, 1), :]
+            for h in range(low // 128):
+                yb[i, h, TOP - 1 : TOP, :] = rim[:, 128 * h : 128 * h + 128]
+                before = yb[i, h, pl.ds(TOP - 1, half, 2), :]
+                middle = yb[i, h, pl.ds(TOP, half, 2), :]
+                after = yb[i, h, pl.ds(TOP + 1, half, 2), :]
+                cz[i, :, 128 * h : 128 * h + 128] = 0.25 * (before + after) + 0.5 * middle
+
+        own_copy(c).start()
+        for d in range(2):
+
+            @pl.when(w_has[d])
+            def _():
+                g_copy(c, w_me, d, True).start()
+
+    def residual_edge():
+        got_x(PASSES)
+        got_y(PASSES, EDGE)
+        put_halo(PASSES, planes, planes)
+        residual_plane(planes, planes, 0)
+        q[planes] = restrict_height(1)[0]
+
+        @pl.when(t_has[1])
+        def _():
+            q_copy().start()
+
+    def residual_part(c):
+        got_y(PASSES, c)
+        if c == 0:
+            put_halo(PASSES, 1, planes + 1)
+            residual_plane(1, planes + 1, 1)
+
+        put_halos(PASSES, c)
+
+        @pl.loop(max(span * c, 2), span * c + span, unroll=4 if c else 7)
+        def _(p):
+            residual_plane(p, p, p - span * c)
+
+        skip = 1 if c == 0 else 0
+        q[span * c + skip : span * c + span] = restrict_height(span)[skip:]
+        if c == 0:
+
+            @pl.when(t_has[0])
+            def _():
+                q_copy().wait_recv()
+
+        @pl.loop(per * c, per * c + per)
+        def _(i):
+            y = 0.25 * (q[2 * i] + q[2 * i + 2]) + 0.5 * q[2 * i + 1]
+            for h in range(low // 128):
+                yb[i, h, pl.ds(TOP, rows), :] = y[:, 128 * h : 128 * h + 128]
+            ycs[c, pl.ds(i - per * c, 1), :] = y[rows - 1 : rows, :]
+
+        @pl.when(w_has[1])
+        def _():
+            c_copy(c).start()
+
+    def forward(turn):
+        for step in range(1, n_width):
+            c = CHUNKS - 1 - (turn - step)
+            if not 0 <= c < CHUNKS:
+                continue
+            for d in range(2):
+                owner = w_me - step if d == 1 else w_me + step
+
+                @pl.when(owner >= 0 if d == 1 else owner < n_width)
+                def _():
+                    g_copy(c, owner, d, False).wait_recv()
+
+                    @pl.when(w_has[d])
+                    def _():
+                        g_copy(c, owner, d, False).start()
+
+    def finish_and_forward(c):
+        finish(c)
+        forward(CHUNKS - 1 - c)
+
     load_v.wait()
     start_x(0)
 
@@ -282,7 +411,6 @@
     ys[0, 1, planes + 1 : planes + 2, :] = va[1, TOP + rows - 1 : TOP + rows, :]
     start_y(0, EDGE)
 
-    order = tuple(range(CHUNKS - 1, -1, -1))
     stores = {}
     for k in range(1, PASSES + 1):
         if k >= 2:
@@ -293,6 +421,8 @@
                     loads[a, c].wait()
         got_x(k - 1)
         got_y(k - 1, EDGE)
+        put_halo(k - 1, planes, planes)
+        put_halo(k - 1, 1, planes + 1)
         smooth_plane(k, planes, planes)
         smooth_plane(k, 1, planes + 1)
         start_x(k)
@@ -305,7 +435,9 @@
             else:
                 got_y(k - 1, c)
 
-            @pl.loop(max(span * c, 2), span * c + span)
+            put_halos(k - 1, c)
+
+            @pl.loop(max(span * c, 2), span * c + span, unroll=4 if c else 7)
             def _(p):
                 smooth_plane(k, p, p)
 
@@ -318,123 +450,19 @@
                     out_sem.at[c],
                 )
                 stores[c].start()
-
-    def q_copy():
-        return pltpu.make_async_remote_copy(
-            src_ref=q.at[planes],
-            dst_ref=q.at[0],
-            send_sem=q_sem.at[0],
-            recv_sem=q_sem.at[1],
-            device_id=t_to[1],
-            device_id_type=MESH,
-        )
-
-    def c_copy(c):
-        part = pl.ds(per * c, per)
-        return pltpu.make_async_remote_copy(
-            src_ref=ycs.at[part, :],
-            dst_ref=ycr.at[part, :],
-            send_sem=c_send.at[c],
-            recv_sem=c_recv.at[c],
-            device_id=w_to[1],
-            device_id_type=MESH,
-        )
-
-    def g_copy(c, owner, d, mine):
-        part = pl.ds(per * c, per)
-        place = coarse.at[part, pl.ds(pl.multiple_of(owner * half, 8), half), :]
-        return pltpu.make_async_remote_copy(
-            src_ref=cz.at[part] if mine else place,
-            dst_ref=place,
-            send_sem=g_send.at[d, owner, c],
-            recv_sem=g_recv.at[owner, c],
-            device_id=w_to[d],
-            device_id_type=MESH,
-        )
-
-    def own_copy(c):
-        part = pl.ds(per * c, per)
-        return pltpu.make_async_copy(
-            cz.at[part],
-            coarse.at[part, pl.ds(pl.multiple_of(w_me * half, 8), half), :],
-            own_sem.at[c],
-        )
-
-    def finish(c):
-        @pl.when(w_has[0])
-        def _():
-            c_copy(c).wait_recv()
-
-        @pl.loop(per * c, per * c + per)
-        def _(i):
-            rim = ycr[pl.ds(i, 1), :]
-            for h in range(low // 128):
-                yb[i, h, TOP - 1 : TOP, :] = rim[:, 128 * h : 128 * h + 128]
-                before = yb[i, h, pl.ds(TOP - 1, half, 2), :]
-                middle = yb[i, h, pl.ds(TOP, half, 2), :]
-                after = yb[i, h, pl.ds(TOP + 1, half, 2), :]
-                cz[i, :, 128 * h : 128 * h + 128] = 0.25 * (before + after) + 0.5 * middle
-
-        own_copy(c).start()
-        for d in range(2):
-
-            @pl.when(w_has[d])
-            def _():
-                g_copy(c, w_me, d, True).start()
-
-    got_x(PASSES)
-    got_y(PASSES, EDGE)
-    residual_plane(planes, planes, 0)
-    q[planes] = restrict_height(1)[0]
-
-    @pl.when(t_has[1])
-    def _():
-        q_copy().start()
-
-    for c in order:
-        got_y(PASSES, c)
-        if c == 0:
-            residual_plane(1, planes + 1, 1)
-
-        @pl.loop(max(span * c, 2), span * c + span)
-        def _(p):
-            residual_plane(p, p, p - span * c)
-
-        skip = 1 if c == 0 else 0
-        q[span * c + skip : span * c + span] = restrict_height(span)[skip:]
-        if c == 0:
-
-            @pl.when(t_has[0])
-            def _():
-                q_copy().wait_recv()
-
-        @pl.loop(per * c, per * c + per)
-        def _(i):
-            y = 0.25 * (q[2 * i] + q[2 * i + 2]) + 0.5 * q[2 * i + 1]
-            for h in range(low // 128):
-                yb[i, h, pl.ds(TOP, rows), :] = y[:, 128 * h : 128 * h + 128]
-            ycs[pl.ds(i, 1), :] = y[rows - 1 : rows, :]
-
-        @pl.when(w_has[1])
-        def _():
-            c_copy(c).start()
-
-        if c < CHUNKS - 1:
-            finish(c + 1)
-    finish(0)
-
-    for step in range(1, n_width):
-        for c in order:
-            for d in range(2):
-                owner = w_me - step if d == 1 else w_me + step
-
-                @pl.when(owner >= 0 if d == 1 else owner < n_width)
-                def _():
-                    g_copy(c, owner, d, False).wait_recv()
-
-                    @pl.when(w_has[d])
-                    def _():
-                        g_copy(c, owner, d, False).start()
+                if c < CHUNKS - 2:
+                    finish_and_forward(c + 2)
+                if c == CHUNKS - 2:
+                    residual_edge()
+                if c < CHUNKS - 1:
+                    residual_part(c + 1)
+
+    residual_part(0)
+    finish_and_forward(1)
+    finish_and_forward(0)
+    for turn in range(CHUNKS, CHUNKS + n_width - 1):
+        forward(turn)
+
 
     for k in (PASSES - 1, PASSES):
         sent_x(k)
@@ -495,8 +523,8 @@
                 pltpu.VMEM((height, low), jnp.bfloat16),
                 pltpu.VMEM((planes + 1, rows, low), f32),
                 pltpu.VMEM((planes // 2, low // 128, rows + TOP, 128), f32),
-                pltpu.VMEM((planes // 2, low), f32),
-                pltpu.VMEM((planes // 2, low), f32),
+                pltpu.VMEM((CHUNKS, 8, low), f32),
+                pltpu.VMEM((CHUNKS, 8, low), f32),
                 pltpu.VMEM((planes // 2, half, low), f32),
                 dma((PASSES + 1, 2)),
                 dma((PASSES + 1, 2)),

time: 91.8 us -> 80.7 us (0.88)
  Pallas kernels: 84.5 us -> 73.4 us
    pallas_call x1, Pallas kernels: 84.5 us -> 73.4 us  [per_device(): pl.pallas_call(functools.partial(kernel, n_tunnel, n_width), out_shape=(j...]
where the time goes in v2:
time: 80.7 us; the launch traced here: 80.5 us
  Pallas kernels  73.4 us (91%)
  local copies, waits for them, and re-layouts  6.48 us (8%)
    pallas_call x1, Pallas kernels, per_device(): pl.pallas_call(functools.partial(kernel, n_tunnel, n_width), out_shape=(j...  73.4 us
    unnamed x4, local copies, waits for them, and re-layouts  6.48 us

profile of v2, /device:TPU:0, one launch (start us, length us, event | category | flops | bytes accessed | tf_op | source)
XLA Modules:
  0.0 80.5 jit_solution(7794250358557194405)
XLA Ops:
  0.6 73.4 %shard_map.59 = (f32[64,32,512]{2,1,0:T(8,128)}, f32[32,64,256]{2,1,0:T(8,128)}) custom-call(f32[64,32,512]{2,1,0:T(8,128)} %source.1, f32[64,32,512]{2,1,0:T(8,128)} %initial.1, f32[64,32,512]{2,1,0:T(8,128)} %diffusivity.1, f32[64,32,512]{2,1,0:T(8,128)} %reaction.1), custom_call_target="tpu_custom_call" | custom-call | tf_op jit(solution)/shard_map/pallas_call | solution.py:505
  74.1 0.0 copy-start
  74.1 5.2 %copy.8 = f32[64,32,512]{2,1,0:T(8,128)} copy(f32[64,32,512]{2,1,0:T(8,128)} %get-tuple-element.4) | data formatting | bytes 8388608
  79.2 0.0 copy-done
  79.2 1.3 %copy.9 = f32[32,64,256]{2,1,0:T(8,128)} copy(f32[32,64,256]{2,1,0:T(8,128)S(1)} %copy-done) | data formatting | bytes 4194304
Async XLA Ops:
  74.1 5.2 %copy-start = (f32[32,64,256]{2,1,0:T(8,128)S(1)}, f32[32,64,256]{2,1,0:T(8,128)}, u32[]{:S(2)}) copy-start(f32[32,64,256]{2,1,0:T(8,128)} %get-tuple-element.5) | copy-start | bytes 6291460
